TPU v7x, 256 devices: a whole 4x4x8 slice. The times are simulated.
256 devices in a mesh: dp: 8 (over x, y_hi), tm: 2 (over y_lo), space: 16 (over z, core).
Axes of the slice: x: 4, y: 4 (y_hi: 2, y_lo: 2; y = y_hi * 2 + y_lo), z: 8, core: 2. Of those that a mesh axis runs over, the one named last changes fastest.
Arguments:
- latents: bfloat16 [256, 4, 256, 512], P(('dp', 'tm', 'space')), parts along dimension 0, may hold values from -36 to 36, as said below
- norm_gain: float32 [512], replicated, may hold values from 0.1 to 1.9
- conv_weight: bfloat16 [3, 3, 3, 512, 256], replicated, may hold values from -0.0546875 to 0.0546875
- skip_weight: bfloat16 [512, 256], replicated, may hold values from -0.25 to 0.25
- cotangent: bfloat16 [256, 16, 4, 16, 256], P(('dp', 'tm'), 'space'), parts along dimension 0, may hold values from -6 to 6
Outputs:
- output: bfloat16 [256, 16, 4, 16, 256], P(('dp', 'tm'), 'space'), parts along dimension 0
- grad_input: bfloat16 [256, 16, 4, 16, 512], P(('dp', 'tm'), 'space'), parts along dimension 0
There are 8 independent parts, one for each index of `dp`. A program takes and returns all parts, laid end to end along the dimension named above; an argument that names none is the same for every part. Nothing has to cross between parts.
Inputs may be any that keep to these rules, and one draw needn't show every extreme that they name: `latents`: each cell and each channel has its own scale.
All inputs are finite; a program needn't handle non-finite values.
Results may differ from a plain program's by a relative error of at most 0.002.
Values may be sent and summed in bfloat16 or wider, within the bound.
A program may use at most 192 MiB of HBM per device.

v0:
```python
import jax
import jax.numpy as jnp
from jax import lax
from jax.sharding import PartitionSpec as P

epsilon = 1e-06


def extended_2(block, sides, width):
    for axis, dim in sides:
        count = lax.axis_size(axis)
        forward = [(i, i + 1) for i in range(count - 1)]
        backward = [(target, source) for source, target in forward]
        low = lax.ppermute(
            lax.slice_in_dim(block, block.shape[dim] - width, None, axis=dim), axis, forward
        )
        high = lax.ppermute(lax.slice_in_dim(block, 0, width, axis=dim), axis, backward)
        block = jnp.concatenate([low, block, high], axis=dim)
    return block


def shifted(value, axis, steps):
    count = lax.axis_size(axis)
    first, last = (max(0, -steps), min(count, count - steps))
    return lax.ppermute(value, axis, [(source, source + steps) for source in range(first, last)])


def activate(x_float, norm_gain):
    mean_sq = jnp.mean(x_float * x_float, axis=-1, keepdims=True)
    inv_rms = lax.rsqrt(mean_sq + epsilon)
    unit_val = x_float * inv_rms
    return (inv_rms, unit_val, unit_val * norm_gain)


def silu_slope(normed):
    sigma_val = jax.nn.sigmoid(normed)
    return sigma_val * (1.0 + normed * (1.0 - sigma_val))


def spread(field):
    widened = extended_2(field, (("space", 2),), 1)
    return jnp.pad(widened, ((0, 0), (1, 1), (0, 0), (0, 0)))


def local(latents, norm_gain, conv_weight, skip_weight, cotangent):
    strips = lax.axis_size("space")
    frame_count, height, width, in_chan = latents.shape
    group_len, single, tile_rows, tile_cols, out_chan = cotangent.shape
    outgoing = latents.reshape(frame_count, height, strips, tile_cols, in_chan).transpose(
        2, 0, 1, 3, 4
    )
    arrived = lax.all_to_all(outgoing, "space", split_axis=0, concat_axis=1, tiled=True)[0]
    inv_rms, unit_val, normed = activate(arrived.astype(jnp.float32), norm_gain)
    hidden = jax.nn.silu(normed).astype(jnp.bfloat16)
    hidden_pad = spread(hidden)
    past_rows = shifted(hidden_pad[group_len - 2 :], "tm", 1)
    extended = jnp.concatenate([past_rows, hidden_pad], 0)
    summed = jnp.dot(arrived.reshape(-1, in_chan), skip_weight, preferred_element_type=jnp.float32)
    for t_tap in range(3):
        for h_tap in range(3):
            for w_tap in range(3):
                window = extended[
                    t_tap : t_tap + group_len, h_tap : h_tap + tile_rows, w_tap : w_tap + tile_cols
                ]
                summed = summed + jnp.dot(
                    window.reshape(-1, in_chan),
                    conv_weight[t_tap, h_tap, w_tap],
                    preferred_element_type=jnp.float32,
                )
    output = summed.astype(jnp.bfloat16).reshape(group_len, 1, tile_rows, tile_cols, out_chan)
    grad_out = cotangent[:, 0]
    grad_pad = spread(grad_out)
    next_rows = shifted(grad_pad[0:2], "tm", -1)
    grad_ext = jnp.concatenate([grad_pad, next_rows], 0)
    contract = (((1,), (1,)), ((), ()))
    grad_skip = lax.dot_general(
        grad_out.reshape(-1, out_chan), skip_weight, contract, preferred_element_type=jnp.float32
    )
    grad_hidden = jnp.zeros((group_len * tile_rows * tile_cols, in_chan), jnp.float32)
    for t_tap in range(3):
        for h_tap in range(3):
            for w_tap in range(3):
                window = grad_ext[
                    2 - t_tap : 2 - t_tap + group_len,
                    2 - h_tap : 2 - h_tap + tile_rows,
                    2 - w_tap : 2 - w_tap + tile_cols,
                ]
                grad_hidden = grad_hidden + lax.dot_general(
                    window.reshape(-1, out_chan),
                    conv_weight[t_tap, h_tap, w_tap],
                    contract,
                    preferred_element_type=jnp.float32,
                )
    grad_unit = (
        grad_hidden.reshape(group_len, tile_rows, tile_cols, in_chan)
        * silu_slope(normed)
        * norm_gain
    )
    grad_input = inv_rms * (
        grad_unit - unit_val * jnp.mean(grad_unit * unit_val, axis=-1, keepdims=True)
    )
    grad_input = grad_input + grad_skip.reshape(group_len, tile_rows, tile_cols, in_chan)
    return (
        output,
        grad_input.astype(jnp.bfloat16).reshape(group_len, 1, tile_rows, tile_cols, in_chan),
    )


def solution(mesh):
    placed = (
        P(("dp", "tm", "space"), None, None, None),
        P(),
        P(),
        P(),
        P(("dp", "tm"), "space", None, None, None),
    )
    return jax.shard_map(
        local,
        mesh=mesh,
        in_specs=placed,
        out_specs=(
            P(("dp", "tm"), "space", None, None, None),
            P(("dp", "tm"), "space", None, None, None),
        ),
        check_vma=False,
    )
```

profile of v0, /device:TPU:1, one launch (start us, length us, event | category | flops | bytes accessed | tf_op | source)
XLA Modules:
  0.0 142.8 jit_solution(12745354876718055685)
XLA Ops:
  0.6 1.8 %fusion.262 = (bf16[16,4,1,256]{3,2,1,0:T(2,128)(2,1)}, bf16[16,4,1,256]{3,2,1,0:T(2,128)(2,1)}) fusion(bf16[16,4,16,256]{3,2,1,0:T(8,128)(2,1)} %bitcast.326), kind=kLoop, calls=%fused_computation.315 | loop fusion | bytes 131072 | tf_op jit(solution)/shard_map/slice | solution.py:15
  2.5 4.9 %collective-permute-start.3 = (bf16[16,4,1,256]{3,2,1,0:T(2,128)(2,1)}, bf16[16,4,1,256]{3,2,1,0:T(2,128)(2,1)S(1)}, u32[]{:S(2)}, u32[]{:S(2)}) collective-permute-start(bf16[16,4,1,256]{3,2,1,0:T(2,128)(2,1)} %get-tuple-element.62), channel_id=1, source_target_pairs={{0,1},{1,2},{2,3},{3,4},{4,5},{5,6},{6,7},{7,8},{8,9},{9,10},{10,1... | collective-permute-start | bytes 98312 | tf_op jit(solution)/shard_map/ppermute | solution.py:14
  7.4 1.9 %collective-permute-start.4 = (bf16[16,4,1,256]{3,2,1,0:T(2,128)(2,1)}, bf16[16,4,1,256]{3,2,1,0:T(2,128)(2,1)S(1)}, u32[]{:S(2)}, u32[]{:S(2)}) collective-permute-start(bf16[16,4,1,256]{3,2,1,0:T(2,128)(2,1)} %get-tuple-element.63), channel_id=1, source_target_pairs={{1,0},{2,1},{3,2},{4,3},{5,4},{6,5},{7,6},{8,7},{9,8},{10,9},{11,1... | collective-permute-start | bytes 98312 | tf_op jit(solution)/shard_map/ppermute | solution.py:17
  9.3 2.3 %copy.12 = bf16[16,1,4,16,512]{4,3,2,1,0:T(8,128)(2,1)} copy(bf16[16,1,4,16,512]{4,3,0,2,1:T(8,128)(2,1)} %bitcast.384) | data formatting | bytes 2097152 | tf_op jit(solution)/shard_map/transpose | solution.py:49
  11.6 9.9 %all-to-all-start = ((bf16[16,1,4,16,512]{4,3,2,1,0:T(8,128)(2,1)}), bf16[16,1,4,16,512]{4,3,2,1,0:T(8,128)(2,1)S(1)}, u32[]{:S(2)}, u32[]{:S(2)}) async-start(bf16[16,1,4,16,512]{4,3,2,1,0:T(8,128)(2,1)} %copy.12), calls=%async_computation | async-start | bytes 2097152 | tf_op jit(solution)/shard_map/all_to_all | solution.py:52
  23.3 2.0 %fusion.64 = bf16[16,6,18,256]{3,2,1,0:T(8,128)(2,1)S(1)} fusion(bf16[16,4,1,256]{3,2,1,0:T(2,128)(2,1)S(1)} %collective-permute-done.4, bf16[16,4,16,256]{3,2,1,0:T(8,128)(2,1)} %bitcast.328, bf16[16,4,1,256]{3,2,1,0:T(2,128)(2,1)S(1)} %collective-permute-done.3), kind=kLoop, calls=%fused_computation.109 | loop fusion | flops 5308416 | bytes 1474560 | tf_op jit(solution)/shard_map/concatenate | solution.py:18
  31.7 1.8 %fusion.118 = f32[1024,512]{1,0:T(8,128)} fusion(bf16[1024,256]{1,0:T(8,128)(2,1)S(1)} %bitcast.367, bf16[3,3,3,512,256]{4,3,2,1,0:T(8,128)(2,1)S(1)} %copy-done.2), kind=kOutput, calls=%fused_computation.169 | convolution fusion | flops 268435456 | bytes 2883584 | tf_op jit(solution)/shard_map/dot_general | solution.py:88
  34.8 1.9 %fusion.122 = f32[1024,512]{1,0:T(8,128)} fusion(bf16[1024,256]{1,0:T(8,128)(2,1)S(1)} %bitcast.366, bf16[3,3,3,512,256]{4,3,2,1,0:T(8,128)(2,1)S(1)} %copy-done.2), kind=kOutput, calls=%fused_computation.173 | convolution fusion | flops 268435456 | bytes 2883584 | tf_op jit(solution)/shard_map/dot_general | solution.py:88
  36.6 1.9 %fusion.126 = f32[1024,512]{1,0:T(8,128)} fusion(bf16[1024,256]{1,0:T(8,128)(2,1)S(1)} %bitcast.365, bf16[3,3,3,512,256]{4,3,2,1,0:T(8,128)(2,1)S(1)} %copy-done.2), kind=kOutput, calls=%fused_computation.177 | convolution fusion | flops 268435456 | bytes 2883584 | tf_op jit(solution)/shard_map/dot_general | solution.py:88
  47.4 1.9 %fusion.154 = f32[1024,512]{1,0:T(8,128)} fusion(bf16[1024,256]{1,0:T(8,128)(2,1)S(1)} %bitcast.359, bf16[3,3,3,512,256]{4,3,2,1,0:T(8,128)(2,1)S(1)} %copy-done.2), kind=kOutput, calls=%fused_computation.205 | convolution fusion | flops 268435456 | bytes 2883584 | tf_op jit(solution)/shard_map/dot_general | solution.py:88
  54.3 1.9 %fusion.158 = f32[1024,512]{1,0:T(8,128)} fusion(bf16[1024,256]{1,0:T(8,128)(2,1)S(1)} %bitcast.381, bf16[3,3,3,512,256]{4,3,2,1,0:T(8,128)(2,1)S(1)} %copy-done.2), kind=kOutput, calls=%fused_computation.209 | convolution fusion | flops 268435456 | bytes 2883584 | tf_op jit(solution)/shard_map/dot_general | solution.py:88
  63.3 1.8 %fusion.178 = f32[1024,512]{1,0:T(8,128)} fusion(bf16[1024,256]{1,0:T(8,128)(2,1)S(1)} %bitcast.376, bf16[3,3,3,512,256]{4,3,2,1,0:T(8,128)(2,1)S(1)} %copy-done.2), kind=kOutput, calls=%fused_computation.229 | convolution fusion | flops 268435456 | bytes 2883584 | tf_op jit(solution)/shard_map/dot_general | solution.py:88
  66.9 1.8 %fusion.186 = f32[1024,512]{1,0:T(8,128)} fusion(bf16[1024,256]{1,0:T(8,128)(2,1)S(1)} %bitcast.374, bf16[3,3,3,512,256]{4,3,2,1,0:T(8,128)(2,1)S(1)} %copy-done.2), kind=kOutput, calls=%fused_computation.237 | convolution fusion | flops 268435456 | bytes 2883584 | tf_op jit(solution)/shard_map/dot_general | solution.py:88
  68.8 1.8 %fusion.190 = f32[1024,512]{1,0:T(8,128)} fusion(bf16[1024,256]{1,0:T(8,128)(2,1)S(1)} %bitcast.373, bf16[3,3,3,512,256]{4,3,2,1,0:T(8,128)(2,1)S(1)} %copy-done.2), kind=kOutput, calls=%fused_computation.241 | convolution fusion | flops 268435456 | bytes 2883584 | tf_op jit(solution)/shard_map/dot_general | solution.py:88
  76.4 19.4 %multiply_reduce_fusion = (f32[1024]{0:T(1024)S(1)}, f32[1024,512]{1,0:T(8,128)}) fusion(f32[512]{0:T(512)S(1)} %copy-done.7, f32[1024]{0:T(1024)S(1)} %rsqrt.13, bf16[16,1,4,16,512]{4,3,2,1,0:T(8,128)(2,1)S(1)} %all-to-all-done, f32[1024,512]{1,0:T(8,128)} %fusion.100, f32[1024,512]{1,0:T(8,128)} %fusion.104, f32[1024,512]{1,0:T(8,128)} %fusion.108, ...), kind=kOutput, calls=%fused_computation.74 | convolution fusion | flops 289405952 | bytes 58468352 | tf_op jit(solution)/shard_map/dot_general | solution.py:88
  96.7 3.6 %collective-permute-start = (bf16[16,4,1,512]{3,2,1,0:T(2,128)(2,1)S(1)}, bf16[16,4,1,512]{3,2,1,0:T(2,128)(2,1)S(1)}, u32[]{:S(2)}, u32[]{:S(2)}) collective-permute-start(bf16[16,4,1,512]{3,2,1,0:T(2,128)(2,1)S(1)} %get-tuple-element.58), channel_id=1, source_target_pairs={{0,1},{1,2},{2,3},{3,4},{4,5},{5,6},{6,7},{7,8},{8,9},{9,10},{10,1... | collective-permute-start | bytes 196616 | tf_op jit(solution)/shard_map/ppermute | solution.py:14
  100.3 1.9 %collective-permute-start.1 = (bf16[16,4,1,512]{3,2,1,0:T(2,128)(2,1)S(1)}, bf16[16,4,1,512]{3,2,1,0:T(2,128)(2,1)S(1)}, u32[]{:S(2)}, u32[]{:S(2)}) collective-permute-start(bf16[16,4,1,512]{3,2,1,0:T(2,128)(2,1)S(1)} %get-tuple-element.59), channel_id=1, source_target_pairs={{1,0},{2,1},{3,2},{4,3},{5,4},{6,5},{7,6},{8,7},{9,8},{10,9},{11,1... | collective-permute-start | bytes 196616 | tf_op jit(solution)/shard_map/ppermute | solution.py:17
  104.4 2.4 %fusion.34 = bf16[16,1,4,16,512]{4,3,2,1,0:T(8,128)(2,1)} fusion(f32[16,4,16,512]{3,2,1,0:T(8,128)S(1)} %bitcast.358, bf16[16,1,4,16,512]{4,3,2,1,0:T(8,128)(2,1)S(1)} %all-to-all-done, f32[16,4,16]{2,1,0:T(4,128)S(1)} %div.25, f32[512]{0:T(512)S(1)} %copy-done.7, f32[16,4,16]{2,1,0:T(4,128)S(1)} %add_rsqrt_fusion, bf16[512,256]{1,0:T(8,128)(2,1)S(1)} %copy-done, ...), kind=kOutput, calls=%fused_computation.76 | convolution fusion | flops 277348352 | bytes 4990976 | tf_op jit(solution)/shard_map/dot_general | solution.py:76
  109.2 4.3 %collective-permute-start.2 = (bf16[2,6,18,512]{3,2,1,0:T(8,128)(2,1)S(1)}, bf16[2,6,18,512]{3,2,1,0:T(8,128)(2,1)S(1)}, u32[]{:S(2)}, u32[]{:S(2)}) collective-permute-start(bf16[2,6,18,512]{3,2,1,0:T(8,128)(2,1)S(1)} %slice.381), channel_id=1, source_target_pairs={{0,16},{1,17},{2,18},{3,19},{4,20},{5,21},{6,22},{7,23},{8,24},{9,... | collective-permute-start | bytes 663560 | tf_op jit(solution)/shard_map/ppermute | solution.py:25
  113.9 2.1 %pad_maximum_fusion = (bf16[16,4,16,512]{3,2,1,0:T(8,128)(2,1)}, bf16[16,4,16,512]{3,2,1,0:T(8,128)(2,1)S(1)}) fusion(bf16[16,4,1,512]{3,2,1,0:T(2,128)(2,1)S(1)} %collective-permute-done.1, bf16[16,4,16,512]{3,2,1,0:T(8,128)(2,1)S(1)} %fusion.17, bf16[16,4,1,512]{3,2,1,0:T(2,128)(2,1)S(1)} %collective-permute-done), kind=kLoop, calls=%fused_computation.127 | loop fusion | flops 4194304 | bytes 3276800 | tf_op jit(solution)/shard_map/concatenate | solution.py:18
  118.7 2.1 %fusion.78 = (bf16[16,4,16,512]{3,2,1,0:T(8,128)(2,1)S(1)}, bf16[16,4,16,512]{3,2,1,0:T(8,128)(2,1)S(1)}, bf16[16,4,16,512]{3,2,1,0:T(8,128)(2,1)S(1)}, bf16[16,...) fusion(bf16[2,6,18,512]{3,2,1,0:T(8,128)(2,1)S(1)} %collective-, ...), kind=kLoop, calls=%fused_computation.123 | loop fusion | flops 12582912 | bytes 13139968 | tf_op jit(solution)/shard_map/concatenate | solution.py:57
  128.2 2.3 %fusion.67 = (bf16[16,4,16,512]{3,2,1,0:T(8,128)(2,1)}, bf16[16,4,16,512]{3,2,1,0:T(8,128)(2,1)S(1)}, bf16[16,4,16,512]{3,2,1,0:T(8,128)(2,1)S(1)}, bf16[16,4,16...) fusion(bf16[2,6,18,512]{3,2,1,0:T(8,128)(2,1)S(1)} %collective-, ...), kind=kLoop, calls=%fused_computation.112 | loop fusion | flops 3145728 | bytes 11042816 | tf_op jit(solution)/shard_map/concatenate | solution.py:57
  135.6 3.5 %fusion.61 = f32[1024,256]{1,0:T(8,128)} fusion(f32[1024,256]{1,0:T(8,128)S(1)} %fusion.116, f32[1024,256]{1,0:T(8,128)S(1)} %fusion.120, f32[1024,256]{1,0:T(8,128)S(1)} %fusion.124, f32[1024,256]{1,0:T(8,128)S(1)} %fusion.128, f32[1024,256]{1,0:T(8,128)S(1)} %fusion.132, f32[1024,256]{1,0:T(8,128)S(1)} %fusion.136, f32[1024,256]{1,0:T(8,128)S(1)} %fusion.140, ...), kind=kOutput, calls=%fused_computation.106 | convolution fusion | flops 274202624 | bytes 25427968 | tf_op jit(solution)/shard_map/dot_general | solution.py:65
  139.0 3.8 %fusion.62 = bf16[1024,256]{1,0:T(8,128)(2,1)} fusion(f32[1024,256]{1,0:T(8,128)} %fusion.102, f32[1024,256]{1,0:T(8,128)} %fusion.106, f32[1024,256]{1,0:T(8,128)} %fusion.110, f32[1024,256]{1,0:T(8,128)} %fusion.61, bf16[1024,512]{1,0:T(8,128)(2,1)} %bitcast.340, bf16[3,3,3,512,256]{4,3,2,1,0:T(8,128)(2,1)S(1)} %bitcast.325), kind=kOutput, calls=%fused_computation.107 | convolution fusion | flops 269746176 | bytes 6029312 | tf_op jit(solution)/shard_map/dot_general | solution.py:65
  (91 shorter events, 58.9 us)
Async XLA Ops:
  0.6 101.6 %copy-start = (bf16[512,256]{1,0:T(8,128)(2,1)S(1)}, bf16[512,256]{1,0:T(8,128)(2,1)}, u32[]{:S(2)}) copy-start(bf16[512,256]{1,0:T(8,128)(2,1)} %param.8) | copy-start | bytes 786436
  2.5 20.8 %collective-permute-start.3 = (bf16[16,4,1,256]{3,2,1,0:T(2,128)(2,1)}, bf16[16,4,1,256]{3,2,1,0:T(2,128)(2,1)S(1)}, u32[]{:S(2)}, u32[]{:S(2)}) collective-permute-start(bf16[16,4,1,256]{3,2,1,0:T(2,128)(2,1)} %get-tuple-element.62), channel_id=1, source_target_pairs={{0,1},{1,2},{2,3},{3,4},{4,5},{5,6},{6,7},{7,8},{8,9},{9,10},{10,1... | collective-permute-start | bytes 98312 | tf_op jit(solution)/shard_map/ppermute | solution.py:14
  7.4 15.9 %collective-permute-start.4 = (bf16[16,4,1,256]{3,2,1,0:T(2,128)(2,1)}, bf16[16,4,1,256]{3,2,1,0:T(2,128)(2,1)S(1)}, u32[]{:S(2)}, u32[]{:S(2)}) collective-permute-start(bf16[16,4,1,256]{3,2,1,0:T(2,128)(2,1)} %get-tuple-element.63), channel_id=1, source_target_pairs={{1,0},{2,1},{3,2},{4,3},{5,4},{6,5},{7,6},{8,7},{9,8},{10,9},{11,1... | collective-permute-start | bytes 98312 | tf_op jit(solution)/shard_map/ppermute | solution.py:17
  11.6 64.3 %all-to-all-start = ((bf16[16,1,4,16,512]{4,3,2,1,0:T(8,128)(2,1)}), bf16[16,1,4,16,512]{4,3,2,1,0:T(8,128)(2,1)S(1)}, u32[]{:S(2)}, u32[]{:S(2)}) async-start(bf16[16,1,4,16,512]{4,3,2,1,0:T(8,128)(2,1)} %copy.12), calls=%async_computation | async-start | bytes 2097152 | tf_op jit(solution)/shard_map/all_to_all | solution.py:52
  21.5 5.3 %copy-start.2 = (bf16[3,3,3,512,256]{4,3,2,1,0:T(8,128)(2,1)S(1)}, bf16[3,3,3,512,256]{4,3,2,1,0:T(8,128)(2,1)}, u32[]{:S(2)}) copy-start(bf16[3,3,3,512,256]{4,3,2,1,0:T(8,128)(2,1)} %param.7) | copy-start | bytes 21233668
  25.5 8.0 %collective-permute-start.5 = (bf16[2,6,18,256]{3,2,1,0:T(8,128)(2,1)S(1)}, bf16[2,6,18,256]{3,2,1,0:T(8,128)(2,1)S(1)}, u32[]{:S(2)}, u32[]{:S(2)}) collective-permute-start(bf16[2,6,18,256]{3,2,1,0:T(8,128)(2,1)S(1)} %slice.424), channel_id=1, source_target_pairs={{16,0},{17,1},{18,2},{19,3},{20,4},{21,5},{22,6},{23,7},{24,8},{25... | collective-permute-start | bytes 331784 | tf_op jit(solution)/shard_map/ppermute | solution.py:25
  28.6 1.8 %copy-start.3 = (bf16[16,1,4,16,256]{4,3,2,1,0:T(8,128)(2,1)S(1)}, bf16[16,1,4,16,256]{4,3,2,1,0:T(8,128)(2,1)}, u32[]{:S(2)}) copy-start(bf16[16,1,4,16,256]{4,3,2,1,0:T(8,128)(2,1)} %param.9) | copy-start | bytes 1572868
  74.2 2.2 %copy-start.7 = (f32[512]{0:T(512)S(1)}, f32[512]{0:T(512)}, u32[]{:S(2)}) copy-start(f32[512]{0:T(512)} %param.6) | copy-start | bytes 6148
  96.7 10.8 %collective-permute-start = (bf16[16,4,1,512]{3,2,1,0:T(2,128)(2,1)S(1)}, bf16[16,4,1,512]{3,2,1,0:T(2,128)(2,1)S(1)}, u32[]{:S(2)}, u32[]{:S(2)}) collective-permute-start(bf16[16,4,1,512]{3,2,1,0:T(2,128)(2,1)S(1)} %get-tuple-element.58), channel_id=1, source_target_pairs={{0,1},{1,2},{2,3},{3,4},{4,5},{5,6},{6,7},{7,8},{8,9},{9,10},{10,1... | collective-permute-start | bytes 196616 | tf_op jit(solution)/shard_map/ppermute | solution.py:14
  100.3 7.2 %collective-permute-start.1 = (bf16[16,4,1,512]{3,2,1,0:T(2,128)(2,1)S(1)}, bf16[16,4,1,512]{3,2,1,0:T(2,128)(2,1)S(1)}, u32[]{:S(2)}, u32[]{:S(2)}) collective-permute-start(bf16[16,4,1,512]{3,2,1,0:T(2,128)(2,1)S(1)} %get-tuple-element.59), channel_id=1, source_target_pairs={{1,0},{2,1},{3,2},{4,3},{5,4},{6,5},{7,6},{8,7},{9,8},{10,9},{11,1... | collective-permute-start | bytes 196616 | tf_op jit(solution)/shard_map/ppermute | solution.py:17
  102.3 2.1 %copy-start.4 = (bf16[16,1,4,16,256]{4,3,2,1,0:T(8,128)(2,1)S(1)}, bf16[16,1,4,16,256]{4,3,2,1,0:T(8,128)(2,1)}, u32[]{:S(2)}) copy-start(bf16[16,1,4,16,256]{4,3,2,1,0:T(8,128)(2,1)} %param.9) | copy-start | bytes 1572868
  102.3 2.1 %copy-start.6 = (f32[1024,512]{1,0:T(8,128)S(1)}, f32[1024,512]{1,0:T(8,128)}, u32[]{:S(2)}) copy-start(f32[1024,512]{1,0:T(8,128)} %get-tuple-element.65) | copy-start | bytes 6291460
  103.7 3.1 %slice-start = ((s8[7077888]{0:T(1024)(128)(4,1)}), s8[4194304]{0:T(1024)(128)(4,1)S(1)}, s32[]{:S(2)}) async-start(s8[7077888]{0:T(1024)(128)(4,1)} %bitcast.324), calls=%async_computation.1 | async-start | bytes 8388608
  104.4 2.7 %slice-start.1 = ((s8[7077888]{0:T(1024)(128)(4,1)}), s8[2883584]{0:T(1024)(128)(4,1)S(1)}, s32[]{:S(2)}) async-start(s8[7077888]{0:T(1024)(128)(4,1)} %bitcast.324), calls=%async_computation.2 | async-start | bytes 5767168
  109.2 9.5 %collective-permute-start.2 = (bf16[2,6,18,512]{3,2,1,0:T(8,128)(2,1)S(1)}, bf16[2,6,18,512]{3,2,1,0:T(8,128)(2,1)S(1)}, u32[]{:S(2)}, u32[]{:S(2)}) collective-permute-start(bf16[2,6,18,512]{3,2,1,0:T(8,128)(2,1)S(1)} %slice.381), channel_id=1, source_target_pairs={{0,16},{1,17},{2,18},{3,19},{4,20},{5,21},{6,22},{7,23},{8,24},{9,... | collective-permute-start | bytes 663560 | tf_op jit(solution)/shard_map/ppermute | solution.py:25
  132.3 2.8 %copy-start.5 = (f32[1024,256]{1,0:T(8,128)S(1)}, f32[1024,256]{1,0:T(8,128)}, u32[]{:S(2)}) copy-start(f32[1024,256]{1,0:T(8,128)} %fusion.263) | copy-start | bytes 3145732
  139.0 3.8 %copy-start.1 = (bf16[512,256]{1,0:T(8,128)(2,1)S(1)}, bf16[512,256]{1,0:T(8,128)(2,1)}, u32[]{:S(2)}) copy-start(bf16[512,256]{1,0:T(8,128)(2,1)} %param.8) | copy-start | bytes 786436
where the time goes:
time: 145 us; the launch traced here: 143 us
  matrix products  91 us (63%)
  starting transfers between devices  27.8 us (19%)
  other arithmetic  16.4 us (11%)
  local copies, waits for them, and re-layouts  5.65 us (4%)
    dot_general x27, matrix products, local(): lax.dot_general(window.reshape(-1, out_chan), conv_weight[t_tap, h_tap, w...  66.2 us
    dot_general x27, matrix products, local(): jnp.dot(window.reshape(-1, in_chan), conv_weight[t_tap, h_tap, w_tap], pr...  21 us
    all_to_all x1, starting transfers between devices, local(): lax.all_to_all(outgoing, 'space', split_axis=0, concat_axis=1, tiled=True)  9.9 us
    ppermute x2, starting transfers between devices, extended_2(): lax.ppermute(lax.slice_in_dim(block, block.shape[dim] - width, None, axis...  8.5 us
    concatenate x4, other arithmetic, extended_2(): block = jnp.concatenate([low, block, high], axis=dim)  6.42 us
    concatenate x3, other arithmetic, local(): extended = jnp.concatenate([past_rows, hidden_pad], 0)  5.66 us
    ppermute x2, starting transfers between devices, shifted(): lax.ppermute(value, axis, [(source, source + steps) for source in range(f...  5.56 us
    ppermute x2, starting transfers between devices, extended_2(): lax.ppermute(lax.slice_in_dim(block, 0, width, axis=dim), axis, backward)  3.84 us
  transfers between devices with their start and end apart: 7, of which 1 were waited for; matrix products, arithmetic and copies ran while one was open for 45% of the time, Pallas kernels for 0%

commit v1 on v0

v1 whole, which is shorter than its diff:
```python
import jax
import jax.numpy as jnp
from jax import lax
from jax.experimental import pallas as pl
from jax.experimental.pallas import tpu as pltpu
from jax.sharding import PartitionSpec as P

MESH = pl.DeviceIdType.MESH
F32 = jnp.float32
BF16 = jnp.bfloat16
EPS = 1e-06
STRIPS = 16
CHIPS = STRIPS // 2
ROWS = 4
COLS = 16
CIN = 512
COUT = 256
CELLS = STRIPS * ROWS * COLS
LINES = STRIPS * ROWS
PAD = 8
NT = (((1,), (1,)), ((), ()))


def activate(x, gain):
    inv = lax.rsqrt(jnp.mean(x * x, axis=-1, keepdims=True) + EPS)
    unit = x * inv
    normed = unit * gain
    sig = 1.0 / (1.0 + jnp.exp(-normed))
    return inv, unit, normed, sig


def mm(a, b):
    return jnp.dot(a, b, preferred_element_type=F32)


def kernel(
    lat, gain_hbm, w_hbm, sk_hbm, cot_hbm, out_hbm, gi_hbm,
    w, sk, gain, cot, arr, arrp, cotn, cedge, chalo, wide, grads, gh, gs,
    hid, pad, edge, halo, hrows, stage, acc, obuf, gbuf,
    local_sem, own_sem, a_send, a_recv, c_send, c_recv, n_send, n_recv,
    h_send, h_recv, p_send, p_recv, out_sem,
):
    me = lax.axis_index("space")
    tm = lax.axis_index("tm")
    chip = me // 2
    other = 1 - tm
    left, right = lax.rem(me + STRIPS - 1, STRIPS), lax.rem(me + 1, STRIPS)
    sides = ((0, right, COLS - 1), (1, left, 0))

    barrier = pltpu.get_barrier_semaphore()
    for k in range(1, STRIPS):
        pl.semaphore_signal(
            barrier, inc=1, device_id={"space": lax.rem(me + k, STRIPS)}, device_id_type=MESH
        )
    for s in (me, left, right):
        pl.semaphore_signal(
            barrier, inc=1, device_id={"space": s, "tm": other}, device_id_type=MESH
        )

    loads = [
        pltpu.make_async_copy(source, target, local_sem.at[i])
        for i, (source, target) in enumerate(
            ((cot_hbm, cot), (sk_hbm, sk), (gain_hbm, gain), (w_hbm, w))
        )
    ]
    for load in loads:
        load.start()
    own = pltpu.make_async_copy(
        lat.at[:, pl.ds(pl.multiple_of(me * COLS, COLS), COLS), :],
        arr.at[pl.ds(me * ROWS, ROWS)],
        own_sem,
    )
    own.start()

    loads[0].wait()
    wide[0:LINES, PAD : PAD + COLS] = cot[...].astype(F32)
    for slot, _, col in sides:
        cedge[slot] = wide[0:LINES, PAD + col, :].astype(BF16)

    pl.semaphore_wait(barrier, STRIPS - 1 + 3)

    started = []
    for slot, target, _ in sides:
        started.append(
            pltpu.make_async_remote_copy(
                src_ref=cedge.at[slot],
                dst_ref=chalo.at[slot, pl.ds(0, LINES)],
                send_sem=c_send.at[slot, 0],
                recv_sem=c_recv.at[slot, 0],
                device_id={"space": target},
                device_id_type=MESH,
            )
        )
        started.append(
            pltpu.make_async_remote_copy(
                src_ref=cedge.at[slot, pl.ds(0, 16)],
                dst_ref=chalo.at[slot, pl.ds(LINES, 16)],
                send_sem=c_send.at[slot, 1],
                recv_sem=c_recv.at[slot, 1],
                device_id={"space": target, "tm": other},
                device_id_type=MESH,
            )
        )
    started.append(
        pltpu.make_async_remote_copy(
            src_ref=cot.at[pl.ds(0, 2 * ROWS)],
            dst_ref=cotn,
            send_sem=n_send,
            recv_sem=n_recv,
            device_id={"tm": other},
            device_id_type=MESH,
        )
    )
    for copy in started:
        copy.start()

    def strip_copy(target, source, i):
        return pltpu.make_async_remote_copy(
            src_ref=lat.at[:, pl.ds(pl.multiple_of(target * COLS, COLS), COLS), :],
            dst_ref=arr.at[pl.ds(source * ROWS, ROWS)],
            send_sem=a_send.at[i],
            recv_sem=a_recv.at[source],
            device_id={"space": target},
            device_id_type=MESH,
        )

    def target_of(i):
        step = i // 2
        if i == 0:
            return chip * 2 + (1 - me % 2)
        step = (i + 1) // 2
        dist = (step + 1) // 2 * (1 if step % 2 else -1)
        return lax.rem(chip + dist + CHIPS, CHIPS) * 2 + lax.rem(me + i, 2)

    sends = [strip_copy(target_of(i), me, i) for i in range(STRIPS - 1)]
    for copy in sends:
        copy.start()

    hid[...] = jnp.zeros_like(hid)
    grads[...] = jnp.zeros_like(grads)
    pad[...] = jnp.zeros_like(pad)
    loads[1].wait()
    loads[2].wait()
    gs[...] = lax.dot_general(
        cot[...].reshape(CELLS, COUT), sk[...], NT, preferred_element_type=F32
    ).reshape(LINES, COLS, CIN)

    for copy in started:
        copy.wait_recv()
    first = jnp.where(tm == 0, 1.0, 0.0)
    second = 1.0 - first
    wide[LINES:, PAD : PAD + COLS] = cotn[...].astype(F32) * first
    has = (jnp.where(me > 0, 1.0, 0.0), jnp.where(me < STRIPS - 1, 1.0, 0.0))
    for slot, sublane in ((0, PAD - 1), (1, PAD + COLS)):
        wide[0:LINES, sublane, :] = chalo[slot, 0:LINES].astype(F32) * has[slot]
        after = chalo[slot, LINES : LINES + 16].astype(F32)[0:8]
        wide[LINES : LINES + 8, sublane, :] = after * (has[slot] * first)

    def spread(f, carry):
        lines = pl.ds(f * ROWS, ROWS)
        for tap in range(3):
            at = PAD + 1 - tap
            grads[f, 1 : 1 + ROWS, :, tap * COUT : (tap + 1) * COUT] = wide[
                lines, at : at + COLS
            ].astype(BF16)
        return carry

    lax.fori_loop(0, STRIPS + 2, spread, 0)

    loads[3].wait()
    gh[...] = jnp.zeros_like(gh)

    def backward(k, carry):
        t, h = k // 3, lax.rem(k, 3)
        part = jnp.zeros((CELLS, CIN), F32)
        for tap in range(3):
            window = grads[
                pl.ds(2 - t, STRIPS), pl.ds(2 - h, ROWS), :, tap * COUT : (tap + 1) * COUT
            ].reshape(CELLS, COUT)
            part = part + lax.dot_general(
                window, w[k, tap * CIN : (tap + 1) * CIN], NT, preferred_element_type=F32
            )
        gh[...] += part.reshape(LINES, COLS, CIN)
        return carry

    lax.fori_loop(0, 9, backward, 0)

    own.wait()

    def put_hidden(i, line, hidden):
        pad[pl.ds(2 * i, 2), PAD : PAD + COLS] = hidden.astype(F32).reshape(2, COLS, CIN)
        f, r = line // 6, lax.rem(line, 6)
        rows = pl.ds(r, 2)
        hid[f, rows, :, 0:CIN] = pad[pl.ds(2 * i, 2), PAD - 1 : PAD - 1 + COLS].astype(BF16)
        hid[f, rows, :, CIN : 2 * CIN] = hidden.reshape(2, COLS, CIN)
        hid[f, rows, :, 2 * CIN :] = pad[pl.ds(2 * i, 2), PAD + 1 : PAD + 1 + COLS].astype(BF16)

    def arrive(k, carry):
        step = (k + 1) // 2
        dist = jnp.where(lax.rem(k, 2) == 1, step, -step)
        c = lax.rem(chip + dist + CHIPS, CHIPS)
        for i in range(2):
            source = 2 * c + i

            @pl.when(source != me)
            def _():
                strip_copy(me, source, 0).wait_recv()

        def lines(i, carry):
            rows = pl.ds(c * 8 + 2 * i, 2)
            x = arr[rows].astype(F32).reshape(2 * COLS, CIN)
            inv, unit, normed, sig = activate(x, gain[...])
            put_hidden(i, (2 * c + 2 + i // 2) * 6 + 1 + lax.rem(i, 2) * 2, (normed * sig).astype(BF16))
            slope = sig * (1.0 + normed * (1.0 - sig))
            gu = gh[rows].reshape(2 * COLS, CIN) * slope * gain[...]
            gx = inv * (gu - unit * jnp.mean(gu * unit, axis=-1, keepdims=True))
            gx = gx + gs[rows].reshape(2 * COLS, CIN)
            gbuf[rows] = gx.astype(BF16).reshape(2, COLS, CIN)
            return carry

        lax.fori_loop(0, 4, lines, 0)
        for slot, target, col in sides:
            edge[slot, c] = pad[:, PAD + col, :]
            edge_copy(slot, target, c).start()
        rows = pl.ds(c * 8, 8)
        pltpu.make_async_copy(gbuf.at[rows], gi_hbm.at[rows], out_sem.at[1 + c]).start()
        return carry

    def edge_copy(slot, target, c):
        return pltpu.make_async_remote_copy(
            src_ref=edge.at[slot, c],
            dst_ref=halo.at[slot, pl.ds((c + 1) * 8, 8)],
            send_sem=h_send.at[slot, c],
            recv_sem=h_recv.at[slot, c],
            device_id={"space": target},
            device_id_type=MESH,
        )

    before = [
        pltpu.make_async_remote_copy(
            src_ref=arr.at[pl.ds(LINES - 8, 8)],
            dst_ref=arrp,
            send_sem=p_send.at[2],
            recv_sem=p_recv.at[2],
            device_id={"tm": other},
            device_id_type=MESH,
        )
    ]
    for slot, target, _ in sides:
        before.append(
            pltpu.make_async_remote_copy(
                src_ref=edge.at[slot, CHIPS - 1],
                dst_ref=halo.at[slot, pl.ds(0, 8)],
                send_sem=p_send.at[slot],
                recv_sem=p_recv.at[slot],
                device_id={"space": target, "tm": other},
                device_id_type=MESH,
            )
        )

    def forward(j, carry):
        lo = jnp.where(j == 0, 0, 2 * j + 1)
        hi = jnp.minimum(2 * j + 3, CHIPS)
        lax.fori_loop(lo, hi, arrive, 0)

        @pl.when(j == 3)
        def _():
            for copy in before:
                copy.start()

        c1 = lax.rem(chip - j + CHIPS, CHIPS)
        c2 = lax.rem(chip + j + 1, CHIPS)
        half = 2 * ROWS * COLS
        stage[0:half] = mm(arr[pl.ds(c1 * 8, 8)].reshape(half, CIN), sk[...])
        stage[half:] = mm(arr[pl.ds(c2 * 8, 8)].reshape(half, CIN), sk[...])

        def taps(t, carry):
            total = stage[...]
            for h in range(3):
                window = jnp.concatenate(
                    [hid[pl.ds(2 * c + t, 2), h : h + ROWS] for c in (c1, c2)], axis=0
                ).reshape(2 * half, 3 * CIN)
                total = total + mm(window, w[3 * t + h])
            stage[...] = total
            return carry

        lax.fori_loop(0, 3, taps, 0)
        acc[pl.ds(c1 * 8, 8)] = stage[0:half].reshape(8, COLS, COUT)
        acc[pl.ds(c2 * 8, 8)] = stage[half:].reshape(8, COLS, COUT)
        return carry

    lax.fori_loop(0, 4, forward, 0)

    before[0].wait_recv()

    def lines_before(i, carry):
        x = arrp[pl.ds(2 * i, 2)].astype(F32).reshape(2 * COLS, CIN)
        _, _, normed, sig = activate(x, gain[...])
        put_hidden(i, (i // 2) * 6 + 1 + lax.rem(i, 2) * 2, (normed * sig * second).astype(BF16))
        return carry

    lax.fori_loop(0, 4, lines_before, 0)
    frame = ROWS * COLS
    both = acc[0 : 2 * ROWS].reshape(2 * frame, COUT)
    one = jnp.zeros((frame, COUT), F32)
    for h in range(3):
        both = both + mm(hid[0:2, h : h + ROWS].reshape(2 * frame, 3 * CIN), w[h])
        one = one + mm(hid[1, h : h + ROWS].reshape(frame, 3 * CIN), w[3 + h])
    acc[0 : 2 * ROWS] = both.reshape(2 * ROWS, COLS, COUT)
    acc[0:ROWS] += one.reshape(ROWS, COLS, COUT)

    for slot, target, _ in sides:

        def wait_edges(c, carry):
            edge_copy(slot, target, c).wait_recv()
            return carry

        lax.fori_loop(0, CHIPS, wait_edges, 0)
        before[1 + slot].wait_recv()
    count = LINES + 8
    for slot, tap, col in ((0, 0, 0), (1, 2, COLS - 1)):
        row = lax.rem(lax.broadcasted_iota(jnp.int32, (count, CIN), 0), ROWS)
        line = lax.broadcasted_iota(jnp.int32, (count, CIN), 0)
        value = halo[slot] * (has[slot] * jnp.where(line < 8, second, 1.0))
        hrows[:, 0:CIN] = jnp.where(row == 0, 0.0, pltpu.roll(value, 1, 0))
        hrows[:, CIN : 2 * CIN] = value
        hrows[:, 2 * CIN :] = jnp.where(row == ROWS - 1, 0.0, pltpu.roll(value, count - 1, 0))
        total = jnp.zeros((LINES, COUT), F32)
        for t in range(3):
            window = hrows[t * ROWS : t * ROWS + LINES].astype(BF16)
            for h in range(3):
                total = total + mm(
                    window[:, h * CIN : (h + 1) * CIN],
                    w[3 * t + h, tap * CIN : (tap + 1) * CIN],
                )
        acc[:, col, :] = acc[:, col, :] + total

    obuf[...] = acc[...].astype(BF16)
    result = pltpu.make_async_copy(obuf, out_hbm, out_sem.at[0])
    result.start()

    for copy in sends + started + before:
        copy.wait_send()
    for slot, target, _ in sides:

        def wait_sent(c, carry):
            edge_copy(slot, target, c).wait_send()
            return carry

        lax.fori_loop(0, CHIPS, wait_sent, 0)

    def wait_out(c, carry):
        rows = pl.ds(c * 8, 8)
        pltpu.make_async_copy(gbuf.at[rows], gi_hbm.at[rows], out_sem.at[1 + c]).wait()
        return carry

    lax.fori_loop(0, CHIPS, wait_out, 0)
    result.wait()


def local(latents, norm_gain, conv_weight, skip_weight, cotangent):
    hbm = pl.BlockSpec(memory_space=pl.ANY)
    dma = pltpu.SemaphoreType.DMA
    out, grad_input = pl.pallas_call(
        kernel,
        out_shape=(
            jax.ShapeDtypeStruct((LINES, COLS, COUT), BF16),
            jax.ShapeDtypeStruct((LINES, COLS, CIN), BF16),
        ),
        in_specs=[hbm] * 5,
        out_specs=(hbm, hbm),
        scratch_shapes=[
            pltpu.VMEM((9, 3 * CIN, COUT), BF16),
            pltpu.VMEM((CIN, COUT), BF16),
            pltpu.VMEM((1, CIN), F32),
            pltpu.VMEM((LINES, COLS, COUT), BF16),
            pltpu.VMEM((LINES, COLS, CIN), BF16),
            pltpu.VMEM((8, COLS, CIN), BF16),
            pltpu.VMEM((8, COLS, COUT), BF16),
            pltpu.VMEM((2, LINES, COUT), BF16),
            pltpu.VMEM((2, LINES + 16, COUT), BF16),
            pltpu.VMEM((LINES + 8, 32, COUT), F32),
            pltpu.VMEM((STRIPS + 2, ROWS + 2, COLS, 3 * COUT), BF16),
            pltpu.VMEM((LINES, COLS, CIN), F32),
            pltpu.VMEM((LINES, COLS, CIN), F32),
            pltpu.VMEM((STRIPS + 2, ROWS + 2, COLS, 3 * CIN), BF16),
            pltpu.VMEM((8, 32, CIN), F32),
            pltpu.VMEM((2, CHIPS, 8, CIN), F32),
            pltpu.VMEM((2, LINES + 8, CIN), F32),
            pltpu.VMEM((LINES + 8, 3 * CIN), F32),
            pltpu.VMEM((4 * ROWS * COLS, COUT), F32),
            pltpu.VMEM((LINES, COLS, COUT), F32),
            pltpu.VMEM((LINES, COLS, COUT), BF16),
            pltpu.VMEM((LINES, COLS, CIN), BF16),
            dma((4,)),
            dma,
            dma((STRIPS - 1,)),
            dma((STRIPS,)),
            dma((2, 2)),
            dma((2, 2)),
            dma,
            dma,
            dma((2, CHIPS)),
            dma((2, CHIPS)),
            dma((3,)),
            dma((3,)),
            dma((1 + CHIPS,)),
        ],
        compiler_params=pltpu.CompilerParams(
            collective_id=0, has_side_effects=True, vmem_limit_bytes=56 * 2**20
        ),
        cost_estimate=pl.CostEstimate(
            flops=2 * CELLS * CIN * COUT * 56, bytes_accessed=11 * 2**20, transcendentals=CELLS * CIN
        ),
    )(
        latents.reshape(ROWS, STRIPS * COLS, CIN),
        norm_gain.reshape(1, CIN),
        conv_weight.reshape(9, 3 * CIN, COUT),
        skip_weight,
        cotangent.reshape(LINES, COLS, COUT),
    )
    return (
        out.reshape(STRIPS, 1, ROWS, COLS, COUT),
        grad_input.reshape(STRIPS, 1, ROWS, COLS, CIN),
    )


def solution(mesh):
    placed = (
        P(("dp", "tm", "space"), None, None, None),
        P(),
        P(),
        P(),
        P(("dp", "tm"), "space", None, None, None),
    )
    return jax.shard_map(
        local,
        mesh=mesh,
        in_specs=placed,
        out_specs=(
            P(("dp", "tm"), "space", None, None, None),
            P(("dp", "tm"), "space", None, None, None),
        ),
        check_vma=False,
    )
```

time: 145 us -> 53.4 us (0.37); the launches traced: 143 us -> 53.2 us
  matrix products: 91 us -> 0 us
  Pallas kernels: 0 us -> 48.4 us
  starting transfers between devices: 27.8 us -> 0 us
  other arithmetic: 16.4 us -> 0 us
  local copies, waits for them, and re-layouts: 5.65 us -> 4.17 us
    dot_general x56 -> x0, matrix products: 91 us -> none  [the longest x27 66.2 us: local(): lax.dot_general(window.reshape(-1, out_chan), conv_weight[t_tap, h_tap, w...]
    pallas_call x0 -> x1, Pallas kernels: none -> 48.4 us  [local(): pl.pallas_call(kernel, out_shape=(jax.ShapeDtypeStruct((LINES, COLS, COUT...]
    ppermute x6 -> x0, starting transfers between devices: 17.9 us -> none  [the longest x2 8.5 us: extended_2(): lax.ppermute(lax.slice_in_dim(block, block.shape[dim] - width, None, axis...]
    concatenate x10 -> x0, other arithmetic: 14.8 us -> none  [the longest x4 6.42 us: extended_2(): block = jnp.concatenate([low, block, high], axis=dim)]
    all_to_all x1 -> x0, starting transfers between devices: 9.9 us -> none  [local(): lax.all_to_all(outgoing, 'space', split_axis=0, concat_axis=1, tiled=True)]
    unnamed x20 -> x2, local copies, waits for them, and re-layouts: 0.31 us -> 4.17 us
    slice x6 -> x0, local copies, waits for them, and re-layouts: 2.89 us -> none  [the longest x2 2.04 us: extended_2(): lax.slice_in_dim(block, block.shape[dim] - width, None, axis=dim)]
    transpose x1 -> x0, local copies, waits for them, and re-layouts: 2.29 us -> none  [local(): latents.reshape(frame_count, height, strips, tile_cols, in_chan)]
  transfers between devices with their start and end apart: 7 -> 0, of which waited for: 1 -> 0; matrix products, arithmetic and copies ran while one was open for 45% -> 0% of each run, Pallas kernels for 0% -> 0%
where the time goes in v1:
time: 53.4 us; the launch traced here: 53.2 us
  Pallas kernels  48.4 us (91%)
  local copies, waits for them, and re-layouts  4.17 us (8%)
  between operations  0.64 us (1%)
    pallas_call x1, Pallas kernels, local(): pl.pallas_call(kernel, out_shape=(jax.ShapeDtypeStruct((LINES, COLS, COUT...  48.4 us
    unnamed x2, local copies, waits for them, and re-layouts  4.17 us

profile of v1, /device:TPU:1, one launch (start us, length us, event | category | flops | bytes accessed | tf_op | source)
XLA Modules:
  0.0 53.2 jit_solution(17017490367225714661)
XLA Ops:
  0.6 48.4 %shard_map.68 = (bf16[64,16,256]{2,1,0:T(8,128)(2,1)}, bf16[64,16,512]{2,1,0:T(8,128)(2,1)}) custom-call(bf16[4,256,512]{2,1,0:T(8,128)(2,1)} %bitcast.13, f32[1,512]{1,0:T(1,128)} %bitcast.15, bf16[9,1536,256]{2,1,0:T(8,128)(2,1)} %bitcast.12, bf16[512,256]{1,0:T(8,128)(2,1)} %sk_hbm.1, bf16[64,16,256]{2,1,0:T(8,128)(2,1)} %bitcast.14), custom_call_target="tpu_custom_call" | custom-call | flops 15032385536 | bytes 11534336 | tf_op jit(solution)/shard_map/pallas_call | solution.py:364
  49.1 1.9 %copy.11 = bf16[16,1,4,16,256]{4,3,2,1,0:T(8,128)(2,1)} copy(bf16[16,1,4,16,256]{4,3,2,1,0:T(8,128)(2,1)} %bitcast.11) | data formatting | bytes 1048576
  50.9 2.3 %copy.12 = bf16[16,1,4,16,512]{4,3,2,1,0:T(8,128)(2,1)} copy(bf16[16,1,4,16,512]{4,3,2,1,0:T(8,128)(2,1)} %bitcast.10) | data formatting | bytes 2097152

commit v2 on v1

--- a/solution.py
+++ b/solution.py
@@ -21,12 +21,10 @@
 NT = (((1,), (1,)), ((), ()))
 
 
-def activate(x, gain):
+def activate(x, half_gain):
     inv = lax.rsqrt(jnp.mean(x * x, axis=-1, keepdims=True) + EPS)
-    unit = x * inv
-    normed = unit * gain
-    sig = 1.0 / (1.0 + jnp.exp(-normed))
-    return inv, unit, normed, sig
+    half = x * inv * half_gain
+    return inv, half, 1.0 + jnp.tanh(half)
 
 
 def mm(a, b):
@@ -34,11 +32,10 @@
 
 
 def kernel(
-    lat, gain_hbm, w_hbm, sk_hbm, cot_hbm, out_hbm, gi_hbm,
-    w, sk, gain, cot, arr, arrp, cotn, cedge, chalo, wide, grads, gh, gs,
-    hid, pad, edge, halo, hrows, stage, acc, obuf, gbuf,
+    lat, gain_hbm, w_hbm, sk_hbm, cot_hbm, w, acc, halo, gbuf,
+    sk, gain, cot, arr, arrp, cotn, cedge, chalo, wide, grads, gh, gs, hid, pad, edge, stage,
     local_sem, own_sem, a_send, a_recv, c_send, c_recv, n_send, n_recv,
-    h_send, h_recv, p_send, p_recv, out_sem,
+    h_send, h_recv, p_send, p_recv,
 ):
     me = lax.axis_index("space")
     tm = lax.axis_index("tm")
@@ -60,7 +57,8 @@
     loads = [
         pltpu.make_async_copy(source, target, local_sem.at[i])
         for i, (source, target) in enumerate(
-            ((cot_hbm, cot), (sk_hbm, sk), (gain_hbm, gain), (w_hbm, w))
+            ((cot_hbm, cot), (sk_hbm, sk), (gain_hbm, gain))
+            + tuple((w_hbm.at[k], w.at[k]) for k in range(9))
         )
     ]
     for load in loads:
@@ -167,11 +165,11 @@
 
     lax.fori_loop(0, STRIPS + 2, spread, 0)
 
-    loads[3].wait()
     gh[...] = jnp.zeros_like(gh)
 
     def backward(k, carry):
         t, h = k // 3, lax.rem(k, 3)
+        pltpu.make_async_copy(w_hbm.at[k], w.at[k], local_sem.at[3 + k]).wait()
         part = jnp.zeros((CELLS, CIN), F32)
         for tap in range(3):
             window = grads[
@@ -187,13 +185,18 @@
 
     own.wait()
 
-    def put_hidden(i, line, hidden):
-        pad[pl.ds(2 * i, 2), PAD : PAD + COLS] = hidden.astype(F32).reshape(2, COLS, CIN)
-        f, r = line // 6, lax.rem(line, 6)
-        rows = pl.ds(r, 2)
-        hid[f, rows, :, 0:CIN] = pad[pl.ds(2 * i, 2), PAD - 1 : PAD - 1 + COLS].astype(BF16)
-        hid[f, rows, :, CIN : 2 * CIN] = hidden.reshape(2, COLS, CIN)
-        hid[f, rows, :, 2 * CIN :] = pad[pl.ds(2 * i, 2), PAD + 1 : PAD + 1 + COLS].astype(BF16)
+    def put_hidden(i, frame, hidden):
+        wide_hidden = hidden.astype(F32).reshape(4, COLS, CIN)
+        f = frame + i // 1
+        rows = pl.ds(1 + 4 * lax.rem(i, 1), 4)
+        pad[pl.ds(4 * i, 4), PAD : PAD + COLS] = wide_hidden
+        hid[f, rows, :, CIN : 2 * CIN] = hidden.reshape(4, COLS, CIN)
+        flat = hidden.astype(F32)
+        col = lax.rem(lax.broadcasted_iota(jnp.int32, (4 * COLS, CIN), 0), COLS)
+        low = jnp.where(col == 0, 0.0, pltpu.roll(flat, 1, 0))
+        high = jnp.where(col == COLS - 1, 0.0, pltpu.roll(flat, 4 * COLS - 1, 0))
+        hid[f, rows, :, 0:CIN] = low.astype(BF16).reshape(4, COLS, CIN)
+        hid[f, rows, :, 2 * CIN :] = high.astype(BF16).reshape(4, COLS, CIN)
 
     def arrive(k, carry):
         step = (k + 1) // 2
@@ -207,23 +210,22 @@
                 strip_copy(me, source, 0).wait_recv()
 
         def lines(i, carry):
-            rows = pl.ds(c * 8 + 2 * i, 2)
-            x = arr[rows].astype(F32).reshape(2 * COLS, CIN)
-            inv, unit, normed, sig = activate(x, gain[...])
-            put_hidden(i, (2 * c + 2 + i // 2) * 6 + 1 + lax.rem(i, 2) * 2, (normed * sig).astype(BF16))
-            slope = sig * (1.0 + normed * (1.0 - sig))
-            gu = gh[rows].reshape(2 * COLS, CIN) * slope * gain[...]
-            gx = inv * (gu - unit * jnp.mean(gu * unit, axis=-1, keepdims=True))
-            gx = gx + gs[rows].reshape(2 * COLS, CIN)
-            gbuf[rows] = gx.astype(BF16).reshape(2, COLS, CIN)
+            rows = pl.ds(c * 8 + 4 * i, 4)
+            x = arr[rows].astype(F32).reshape(4 * COLS, CIN)
+            half_gain = 0.5 * gain[...]
+            inv, half, twice = activate(x, half_gain)
+            hidden = half * twice
+            put_hidden(i, c * 2 + 2, hidden.astype(BF16))
+            gu = gh[rows].reshape(4 * COLS, CIN) * half_gain * (twice + hidden * (2.0 - twice))
+            along = jnp.mean(gu * x, axis=-1, keepdims=True) * (inv * inv)
+            gx = inv * (gu - x * along) + gs[rows].reshape(4 * COLS, CIN)
+            gbuf[rows] = gx.astype(BF16).reshape(4, COLS, CIN)
             return carry
 
-        lax.fori_loop(0, 4, lines, 0)
+        lax.fori_loop(0, 2, lines, 0, unroll=2)
         for slot, target, col in sides:
             edge[slot, c] = pad[:, PAD + col, :]
             edge_copy(slot, target, c).start()
-        rows = pl.ds(c * 8, 8)
-        pltpu.make_async_copy(gbuf.at[rows], gi_hbm.at[rows], out_sem.at[1 + c]).start()
         return carry
 
     def edge_copy(slot, target, c):
@@ -294,12 +296,12 @@
     before[0].wait_recv()
 
     def lines_before(i, carry):
-        x = arrp[pl.ds(2 * i, 2)].astype(F32).reshape(2 * COLS, CIN)
-        _, _, normed, sig = activate(x, gain[...])
-        put_hidden(i, (i // 2) * 6 + 1 + lax.rem(i, 2) * 2, (normed * sig * second).astype(BF16))
+        x = arrp[pl.ds(4 * i, 4)].astype(F32).reshape(4 * COLS, CIN)
+        _, half, twice = activate(x, 0.5 * gain[...])
+        put_hidden(i, 0, (half * twice * second).astype(BF16))
         return carry
 
-    lax.fori_loop(0, 4, lines_before, 0)
+    lax.fori_loop(0, 2, lines_before, 0)
     frame = ROWS * COLS
     both = acc[0 : 2 * ROWS].reshape(2 * frame, COUT)
     one = jnp.zeros((frame, COUT), F32)
@@ -317,6 +319,24 @@
 
         lax.fori_loop(0, CHIPS, wait_edges, 0)
         before[1 + slot].wait_recv()
+    for copy in sends + started + before:
+        copy.wait_send()
+    for slot, target, _ in sides:
+
+        def wait_sent(c, carry):
+            edge_copy(slot, target, c).wait_send()
+            return carry
+
+        lax.fori_loop(0, CHIPS, wait_sent, 0)
+
+
+def finish(w, acc, halo, gbuf, out_hbm, gi_hbm, hrows, full, obuf, sem):
+    ready = pltpu.make_async_copy(gbuf, gi_hbm, sem.at[0])
+    ready.start()
+    full[...] = acc[...]
+    me = lax.axis_index("space")
+    second = jnp.where(lax.axis_index("tm") == 0, 0.0, 1.0)
+    has = (jnp.where(me > 0, 1.0, 0.0), jnp.where(me < STRIPS - 1, 1.0, 0.0))
     count = LINES + 8
     for slot, tap, col in ((0, 0, 0), (1, 2, COLS - 1)):
         row = lax.rem(lax.broadcasted_iota(jnp.int32, (count, CIN), 0), ROWS)
@@ -333,44 +353,30 @@
                     window[:, h * CIN : (h + 1) * CIN],
                     w[3 * t + h, tap * CIN : (tap + 1) * CIN],
                 )
-        acc[:, col, :] = acc[:, col, :] + total
-
-    obuf[...] = acc[...].astype(BF16)
-    result = pltpu.make_async_copy(obuf, out_hbm, out_sem.at[0])
+        full[:, col, :] = full[:, col, :] + total
+
+    obuf[...] = full[...].astype(BF16)
+    result = pltpu.make_async_copy(obuf, out_hbm, sem.at[1])
     result.start()
-
-    for copy in sends + started + before:
-        copy.wait_send()
-    for slot, target, _ in sides:
-
-        def wait_sent(c, carry):
-            edge_copy(slot, target, c).wait_send()
-            return carry
-
-        lax.fori_loop(0, CHIPS, wait_sent, 0)
-
-    def wait_out(c, carry):
-        rows = pl.ds(c * 8, 8)
-        pltpu.make_async_copy(gbuf.at[rows], gi_hbm.at[rows], out_sem.at[1 + c]).wait()
-        return carry
-
-    lax.fori_loop(0, CHIPS, wait_out, 0)
+    ready.wait()
     result.wait()
 
 
 def local(latents, norm_gain, conv_weight, skip_weight, cotangent):
     hbm = pl.BlockSpec(memory_space=pl.ANY)
     dma = pltpu.SemaphoreType.DMA
-    out, grad_input = pl.pallas_call(
+    vmem = pl.BlockSpec(memory_space=pltpu.VMEM)
+    parts = pl.pallas_call(
         kernel,
         out_shape=(
-            jax.ShapeDtypeStruct((LINES, COLS, COUT), BF16),
-            jax.ShapeDtypeStruct((LINES, COLS, CIN), BF16),
+            pltpu.VMEM((9, 3 * CIN, COUT), BF16),
+            pltpu.VMEM((LINES, COLS, COUT), F32),
+            pltpu.VMEM((2, LINES + 8, CIN), F32),
+            pltpu.VMEM((LINES, COLS, CIN), BF16),
         ),
         in_specs=[hbm] * 5,
-        out_specs=(hbm, hbm),
+        out_specs=(vmem,) * 4,
         scratch_shapes=[
-            pltpu.VMEM((9, 3 * CIN, COUT), BF16),
             pltpu.VMEM((CIN, COUT), BF16),
             pltpu.VMEM((1, CIN), F32),
             pltpu.VMEM((LINES, COLS, COUT), BF16),
@@ -386,13 +392,8 @@
             pltpu.VMEM((STRIPS + 2, ROWS + 2, COLS, 3 * CIN), BF16),
             pltpu.VMEM((8, 32, CIN), F32),
             pltpu.VMEM((2, CHIPS, 8, CIN), F32),
-            pltpu.VMEM((2, LINES + 8, CIN), F32),
-            pltpu.VMEM((LINES + 8, 3 * CIN), F32),
             pltpu.VMEM((4 * ROWS * COLS, COUT), F32),
-            pltpu.VMEM((LINES, COLS, COUT), F32),
-            pltpu.VMEM((LINES, COLS, COUT), BF16),
-            pltpu.VMEM((LINES, COLS, CIN), BF16),
-            dma((4,)),
+            dma((3 + 9,)),
             dma,
             dma((STRIPS - 1,)),
             dma((STRIPS,)),
@@ -404,10 +405,9 @@
             dma((2, CHIPS)),
             dma((3,)),
             dma((3,)),
-            dma((1 + CHIPS,)),
         ],
         compiler_params=pltpu.CompilerParams(
-            collective_id=0, has_side_effects=True, vmem_limit_bytes=56 * 2**20
+            collective_id=0, has_side_effects=True, vmem_limit_bytes=53 * 2**20
         ),
         cost_estimate=pl.CostEstimate(
             flops=2 * CELLS * CIN * COUT * 56, bytes_accessed=11 * 2**20, transcendentals=CELLS * CIN
@@ -419,6 +419,22 @@
         skip_weight,
         cotangent.reshape(LINES, COLS, COUT),
     )
+    out, grad_input = pl.pallas_call(
+        finish,
+        out_shape=(
+            jax.ShapeDtypeStruct((LINES, COLS, COUT), BF16),
+            jax.ShapeDtypeStruct((LINES, COLS, CIN), BF16),
+        ),
+        in_specs=[vmem] * 4,
+        out_specs=(hbm, hbm),
+        scratch_shapes=[
+            pltpu.VMEM((LINES + 8, 3 * CIN), F32),
+            pltpu.VMEM((LINES, COLS, COUT), F32),
+            pltpu.VMEM((LINES, COLS, COUT), BF16),
+            dma((2,)),
+        ],
+        compiler_params=pltpu.CompilerParams(vmem_limit_bytes=16 * 2**20),
+    )(*parts)
     return (
         out.reshape(STRIPS, 1, ROWS, COLS, COUT),
         grad_input.reshape(STRIPS, 1, ROWS, COLS, CIN),

time: 53.4 us -> 43.3 us (0.81)
  the two profiles are of different devices: /device:TPU:1 before, /device:TPU:68 now
where the time goes in v2:
time: 43.3 us; the launch traced here: 43.2 us
  Pallas kernels  42.6 us (98%)
  between operations  0.64 us (1%)
    pallas_call x1, Pallas kernels, local(): pl.pallas_call(kernel, out_shape=(pltpu.VMEM((9, 3 * CIN, COUT), BF16), p...  40.8 us
    pallas_call x1, Pallas kernels, local(): pl.pallas_call(finish, out_shape=(jax.ShapeDtypeStruct((LINES, COLS, COUT...  1.85 us

profile of v2, /device:TPU:68, one launch (start us, length us, event | category | flops | bytes accessed | tf_op | source)
XLA Modules:
  0.0 43.2 jit_solution(2174184103061294080)
XLA Ops:
  0.6 40.8 %shard_map.68 = (bf16[9,1536,256]{2,1,0:T(8,128)(2,1)S(1)}, f32[64,16,256]{2,1,0:T(8,128)S(1)}, f32[2,72,512]{2,1,0:T(8,128)S(1)}, bf16[64,16,512]{2,1,0:T(8,128)(2,1)S(1)}) custom-call(bf16[4,256,512]{2,1,0:T(8,128)(2,1)} %bitcast.11, f32[1,512]{1,0:T(1,128)} %bitcast.15, bf16[9,1536,256]{2,1,0:T(8,128)(2,1)} %bitcast.10, bf16[512,256]{1,0:T(8,128)(2,1)} %sk_hbm.1, ...), custom_call_target="tpu_custom_call" | custom-call | flops 15032385536 | bytes 11534336 | tf_op jit(solution)/shard_map/pallas_call | solution.py:369
  41.4 1.8 %shard_map.69 = (bf16[64,16,256]{2,1,0:T(8,128)(2,1)}, bf16[64,16,512]{2,1,0:T(8,128)(2,1)}) custom-call(bf16[9,1536,256]{2,1,0:T(8,128)(2,1)S(1)} %get-tuple-element.8.w, f32[64,16,256]{2,1,0:T(8,128)S(1)} %get-tuple-element.9.acc, f32[2,72,512]{2,1,0:T(8,128)S(1)} %get-tuple-element.10.halo, bf16[64,16,512]{2,1,0:T(8,128)(2,1)S(1)} %get-tuple-element.11.gbuf), custom_call_target="tpu_custom_call" | custom-call | tf_op jit(solution)/shard_map/pallas_call | solution.py:422

commit v3 on v2

--- a/solution.py
+++ b/solution.py
@@ -31,9 +31,22 @@
     return jnp.dot(a, b, preferred_element_type=F32)
 
 
+def put_hidden(hid, frame, hidden):
+    count = hidden.shape[0] // (ROWS * COLS)
+    rows = pl.ds(1, ROWS)
+    frames = pl.ds(frame, count)
+    shape = (count, ROWS, COLS, CIN)
+    hid[frames, rows, :, CIN : 2 * CIN] = hidden.astype(BF16).reshape(shape)
+    col = lax.rem(lax.broadcasted_iota(jnp.int32, hidden.shape, 0), COLS)
+    low = jnp.where(col == 0, 0.0, pltpu.roll(hidden, 1, 0))
+    high = jnp.where(col == COLS - 1, 0.0, pltpu.roll(hidden, hidden.shape[0] - 1, 0))
+    hid[frames, rows, :, 0:CIN] = low.astype(BF16).reshape(shape)
+    hid[frames, rows, :, 2 * CIN :] = high.astype(BF16).reshape(shape)
+
+
 def kernel(
-    lat, gain_hbm, w_hbm, sk_hbm, cot_hbm, w, acc, halo, gbuf,
-    sk, gain, cot, arr, arrp, cotn, cedge, chalo, wide, grads, gh, gs, hid, pad, edge, stage,
+    lat, gain_hbm, w_hbm, sk_hbm, cot_hbm, w, acc, hidp, halo, gbuf,
+    sk, gain, cot, arr, arrp, cotn, cedge, chalo, wide, grads, gh, gs, hid, pad, edge, edge_out,
     local_sem, own_sem, a_send, a_recv, c_send, c_recv, n_send, n_recv,
     h_send, h_recv, p_send, p_recv,
 ):
@@ -134,9 +147,10 @@
     for copy in sends:
         copy.start()
 
-    hid[...] = jnp.zeros_like(hid)
-    grads[...] = jnp.zeros_like(grads)
-    pad[...] = jnp.zeros_like(pad)
+    for ref in (hid, grads, hidp):
+        for r in (0, ROWS + 1):
+            ref[:, r] = jnp.zeros((ref.shape[0],) + ref.shape[2:], BF16)
+    acc[...] = jnp.zeros_like(acc)
     loads[1].wait()
     loads[2].wait()
     gs[...] = lax.dot_general(
@@ -146,7 +160,6 @@
     for copy in started:
         copy.wait_recv()
     first = jnp.where(tm == 0, 1.0, 0.0)
-    second = 1.0 - first
     wide[LINES:, PAD : PAD + COLS] = cotn[...].astype(F32) * first
     has = (jnp.where(me > 0, 1.0, 0.0), jnp.where(me < STRIPS - 1, 1.0, 0.0))
     for slot, sublane in ((0, PAD - 1), (1, PAD + COLS)):
@@ -185,23 +198,10 @@
 
     own.wait()
 
-    def put_hidden(i, frame, hidden):
-        wide_hidden = hidden.astype(F32).reshape(4, COLS, CIN)
-        f = frame + i // 1
-        rows = pl.ds(1 + 4 * lax.rem(i, 1), 4)
-        pad[pl.ds(4 * i, 4), PAD : PAD + COLS] = wide_hidden
-        hid[f, rows, :, CIN : 2 * CIN] = hidden.reshape(4, COLS, CIN)
-        flat = hidden.astype(F32)
-        col = lax.rem(lax.broadcasted_iota(jnp.int32, (4 * COLS, CIN), 0), COLS)
-        low = jnp.where(col == 0, 0.0, pltpu.roll(flat, 1, 0))
-        high = jnp.where(col == COLS - 1, 0.0, pltpu.roll(flat, 4 * COLS - 1, 0))
-        hid[f, rows, :, 0:CIN] = low.astype(BF16).reshape(4, COLS, CIN)
-        hid[f, rows, :, 2 * CIN :] = high.astype(BF16).reshape(4, COLS, CIN)
-
-    def arrive(k, carry):
-        step = (k + 1) // 2
-        dist = jnp.where(lax.rem(k, 2) == 1, step, -step)
-        c = lax.rem(chip + dist + CHIPS, CHIPS)
+    def chip_at(dist):
+        return lax.rem(chip + dist + CHIPS, CHIPS)
+
+    def await_chip(c):
         for i in range(2):
             source = 2 * c + i
 
@@ -209,34 +209,48 @@
             def _():
                 strip_copy(me, source, 0).wait_recv()
 
-        def lines(i, carry):
-            rows = pl.ds(c * 8 + 4 * i, 4)
-            x = arr[rows].astype(F32).reshape(4 * COLS, CIN)
-            half_gain = 0.5 * gain[...]
+    def arrive(c):
+        half_gain = 0.5 * gain[...]
+        for i in range(2):
+            rows = pl.ds(c * 8 + ROWS * i, ROWS)
+            x = arr[rows].astype(F32).reshape(ROWS * COLS, CIN)
             inv, half, twice = activate(x, half_gain)
-            hidden = half * twice
-            put_hidden(i, c * 2 + 2, hidden.astype(BF16))
-            gu = gh[rows].reshape(4 * COLS, CIN) * half_gain * (twice + hidden * (2.0 - twice))
+            exact = half * twice
+            hidden = exact.astype(BF16).astype(F32)
+            pad[ROWS * i : ROWS * i + ROWS] = hidden.reshape(ROWS, COLS, CIN)
+            put_hidden(hid, 2 * c + i, hidden)
+            gu = gh[rows].reshape(ROWS * COLS, CIN) * half_gain * (twice + exact * (2.0 - twice))
             along = jnp.mean(gu * x, axis=-1, keepdims=True) * (inv * inv)
-            gx = inv * (gu - x * along) + gs[rows].reshape(4 * COLS, CIN)
-            gbuf[rows] = gx.astype(BF16).reshape(4, COLS, CIN)
+            gx = inv * (gu - x * along) + gs[rows].reshape(ROWS * COLS, CIN)
+            gbuf[rows] = gx.astype(BF16).reshape(ROWS, COLS, CIN)
+        for slot, _, col in sides:
+            edge[slot, pl.ds(c * 8, 8)] = pad[:, col, :]
+
+    half = 2 * ROWS * COLS
+
+    def add(line, value):
+        acc[pl.ds(line, 8)] += value.reshape(8, COLS, COUT)
+
+    def forward(chips):
+        def both(values):
+            return values[0] if len(values) == 1 else jnp.concatenate(values, axis=0)
+
+        shortcut = mm(both([arr[pl.ds(c * 8, 8)].reshape(half, CIN) for c in chips]), sk[...])
+        for i, c in enumerate(chips):
+            add(c * 8, shortcut[i * half : (i + 1) * half])
+
+        def taps(t, carry):
+            total = jnp.zeros((len(chips) * half, COUT), F32)
+            for h in range(3):
+                window = both(
+                    [hid[pl.ds(2 * c, 2), h : h + ROWS].reshape(half, 3 * CIN) for c in chips]
+                )
+                total = total + mm(window, w[3 * t + h])
+            for i, c in enumerate(chips):
+                add((2 * c + 2 - t) * ROWS, total[i * half : (i + 1) * half])
             return carry
 
-        lax.fori_loop(0, 2, lines, 0, unroll=2)
-        for slot, target, col in sides:
-            edge[slot, c] = pad[:, PAD + col, :]
-            edge_copy(slot, target, c).start()
-        return carry
-
-    def edge_copy(slot, target, c):
-        return pltpu.make_async_remote_copy(
-            src_ref=edge.at[slot, c],
-            dst_ref=halo.at[slot, pl.ds((c + 1) * 8, 8)],
-            send_sem=h_send.at[slot, c],
-            recv_sem=h_recv.at[slot, c],
-            device_id={"space": target},
-            device_id_type=MESH,
-        )
+        lax.fori_loop(0, 3, taps, 0)
 
     before = [
         pltpu.make_async_remote_copy(
@@ -248,11 +262,22 @@
             device_id_type=MESH,
         )
     ]
+    columns = []
     for slot, target, _ in sides:
+        columns.append(
+            pltpu.make_async_remote_copy(
+                src_ref=edge_out.at[slot],
+                dst_ref=halo.at[slot, pl.ds(0, LINES)],
+                send_sem=h_send.at[slot],
+                recv_sem=h_recv.at[slot],
+                device_id={"space": target},
+                device_id_type=MESH,
+            )
+        )
         before.append(
             pltpu.make_async_remote_copy(
-                src_ref=edge.at[slot, CHIPS - 1],
-                dst_ref=halo.at[slot, pl.ds(0, 8)],
+                src_ref=edge_out.at[slot, pl.ds(LINES - 16, 16)],
+                dst_ref=halo.at[slot, pl.ds(LINES, 16)],
                 send_sem=p_send.at[slot],
                 recv_sem=p_recv.at[slot],
                 device_id={"space": target, "tm": other},
@@ -260,101 +285,95 @@
             )
         )
 
-    def forward(j, carry):
-        lo = jnp.where(j == 0, 0, 2 * j + 1)
-        hi = jnp.minimum(2 * j + 3, CHIPS)
-        lax.fori_loop(lo, hi, arrive, 0)
-
-        @pl.when(j == 3)
+    await_chip(chip)
+    arrive(chip)
+    forward([chip])
+
+    def pair(j, carry):
+        def one(i, carry):
+            c = chip_at(jnp.where(i == 0, j, -j))
+            await_chip(c)
+            arrive(c)
+            return carry
+
+        lax.fori_loop(0, 2, one, 0)
+
+        @pl.when(j < 3)
         def _():
-            for copy in before:
-                copy.start()
-
-        c1 = lax.rem(chip - j + CHIPS, CHIPS)
-        c2 = lax.rem(chip + j + 1, CHIPS)
-        half = 2 * ROWS * COLS
-        stage[0:half] = mm(arr[pl.ds(c1 * 8, 8)].reshape(half, CIN), sk[...])
-        stage[half:] = mm(arr[pl.ds(c2 * 8, 8)].reshape(half, CIN), sk[...])
-
-        def taps(t, carry):
-            total = stage[...]
-            for h in range(3):
-                window = jnp.concatenate(
-                    [hid[pl.ds(2 * c + t, 2), h : h + ROWS] for c in (c1, c2)], axis=0
-                ).reshape(2 * half, 3 * CIN)
-                total = total + mm(window, w[3 * t + h])
-            stage[...] = total
-            return carry
-
-        lax.fori_loop(0, 3, taps, 0)
-        acc[pl.ds(c1 * 8, 8)] = stage[0:half].reshape(8, COLS, COUT)
-        acc[pl.ds(c2 * 8, 8)] = stage[half:].reshape(8, COLS, COUT)
+            forward([chip_at(j), chip_at(-j)])
+
         return carry
 
-    lax.fori_loop(0, 4, forward, 0)
-
+    lax.fori_loop(1, 4, pair, 0)
+    last = chip_at(4)
+    await_chip(last)
+    before[0].start()
+    arrive(last)
+    for slot in range(2):
+        edge_out[slot] = edge[slot].astype(BF16)
+    for copy in columns + before[1:]:
+        copy.start()
+    forward([chip_at(3), chip_at(-3), last])
     before[0].wait_recv()
-
-    def lines_before(i, carry):
-        x = arrp[pl.ds(4 * i, 4)].astype(F32).reshape(4 * COLS, CIN)
-        _, half, twice = activate(x, 0.5 * gain[...])
-        put_hidden(i, 0, (half * twice * second).astype(BF16))
-        return carry
-
-    lax.fori_loop(0, 2, lines_before, 0)
-    frame = ROWS * COLS
-    both = acc[0 : 2 * ROWS].reshape(2 * frame, COUT)
-    one = jnp.zeros((frame, COUT), F32)
-    for h in range(3):
-        both = both + mm(hid[0:2, h : h + ROWS].reshape(2 * frame, 3 * CIN), w[h])
-        one = one + mm(hid[1, h : h + ROWS].reshape(frame, 3 * CIN), w[3 + h])
-    acc[0 : 2 * ROWS] = both.reshape(2 * ROWS, COLS, COUT)
-    acc[0:ROWS] += one.reshape(ROWS, COLS, COUT)
-
-    for slot, target, _ in sides:
-
-        def wait_edges(c, carry):
-            edge_copy(slot, target, c).wait_recv()
-            return carry
-
-        lax.fori_loop(0, CHIPS, wait_edges, 0)
-        before[1 + slot].wait_recv()
-    for copy in sends + started + before:
+    second = jnp.where(tm == 0, 0.0, 1.0)
+    for i in range(2):
+        x = arrp[ROWS * i : ROWS * i + ROWS].astype(F32).reshape(ROWS * COLS, CIN)
+        _, value, twice = activate(x, 0.5 * gain[...])
+        put_hidden(hidp, i, (value * twice).astype(BF16).astype(F32) * second)
+    for copy in columns + before[1:]:
+        copy.wait_recv()
+
+    for copy in sends + started + columns + before:
         copy.wait_send()
-    for slot, target, _ in sides:
-
-        def wait_sent(c, carry):
-            edge_copy(slot, target, c).wait_send()
-            return carry
-
-        lax.fori_loop(0, CHIPS, wait_sent, 0)
-
-
-def finish(w, acc, halo, gbuf, out_hbm, gi_hbm, hrows, full, obuf, sem):
+
+
+def finish(w, acc, hidp, halo, gbuf, out_hbm, gi_hbm, hrows, full, obuf, sem):
     ready = pltpu.make_async_copy(gbuf, gi_hbm, sem.at[0])
     ready.start()
-    full[...] = acc[...]
     me = lax.axis_index("space")
     second = jnp.where(lax.axis_index("tm") == 0, 0.0, 1.0)
     has = (jnp.where(me > 0, 1.0, 0.0), jnp.where(me < STRIPS - 1, 1.0, 0.0))
+    full[...] = acc[0:LINES]
+
     count = LINES + 8
-    for slot, tap, col in ((0, 0, 0), (1, 2, COLS - 1)):
-        row = lax.rem(lax.broadcasted_iota(jnp.int32, (count, CIN), 0), ROWS)
-        line = lax.broadcasted_iota(jnp.int32, (count, CIN), 0)
-        value = halo[slot] * (has[slot] * jnp.where(line < 8, second, 1.0))
-        hrows[:, 0:CIN] = jnp.where(row == 0, 0.0, pltpu.roll(value, 1, 0))
-        hrows[:, CIN : 2 * CIN] = value
-        hrows[:, 2 * CIN :] = jnp.where(row == ROWS - 1, 0.0, pltpu.roll(value, count - 1, 0))
-        total = jnp.zeros((LINES, COUT), F32)
-        for t in range(3):
-            window = hrows[t * ROWS : t * ROWS + LINES].astype(BF16)
-            for h in range(3):
-                total = total + mm(
-                    window[:, h * CIN : (h + 1) * CIN],
-                    w[3 * t + h, tap * CIN : (tap + 1) * CIN],
+    line = lax.broadcasted_iota(jnp.int32, (count, CIN), 0)
+    row = lax.rem(line, ROWS)
+    for slot in range(2):
+        got = halo[slot].astype(F32)
+        value = jnp.concatenate([got[LINES + 8 :] * second, got[0:LINES]], axis=0) * has[slot]
+        hrows[slot, :, 0:CIN] = jnp.where(row == 0, 0.0, pltpu.roll(value, 1, 0))
+        hrows[slot, :, CIN : 2 * CIN] = value
+        hrows[slot, :, 2 * CIN :] = jnp.where(
+            row == ROWS - 1, 0.0, pltpu.roll(value, count - 1, 0)
+        )
+
+    frame = ROWS * COLS
+    shares = [jnp.zeros((n, COUT), F32) for n in (2 * frame, frame, LINES, LINES)]
+    for t in range(3):
+        sides = [hrows[slot, t * ROWS : t * ROWS + LINES].astype(BF16) for slot in range(2)]
+        for h in range(3):
+            for c in range(3):
+                takes = []
+                if t < 2:
+                    lines = hidp[t:2, h : h + ROWS, :, c * CIN : (c + 1) * CIN]
+                    takes.append((t, lines.reshape((2 - t) * frame, CIN)))
+                if c != 1:
+                    takes.append((2 + c // 2, sides[c // 2][:, h * CIN : (h + 1) * CIN]))
+                if not takes:
+                    continue
+                product = mm(
+                    takes[0][1] if len(takes) == 1 else jnp.concatenate([v for _, v in takes], 0),
+                    w[3 * t + h, c * CIN : (c + 1) * CIN],
                 )
-        full[:, col, :] = full[:, col, :] + total
-
+                start = 0
+                for share, v in takes:
+                    shares[share] = shares[share] + product[start : start + v.shape[0]]
+                    start += v.shape[0]
+
+    full[0:8] += shares[0].reshape(8, COLS, COUT)
+    full[0:ROWS] += shares[1].reshape(ROWS, COLS, COUT)
+    for col, share in ((0, shares[2]), (COLS - 1, shares[3])):
+        full[:, col, :] = full[:, col, :] + share
     obuf[...] = full[...].astype(BF16)
     result = pltpu.make_async_copy(obuf, out_hbm, sem.at[1])
     result.start()
@@ -370,12 +389,13 @@
         kernel,
         out_shape=(
             pltpu.VMEM((9, 3 * CIN, COUT), BF16),
-            pltpu.VMEM((LINES, COLS, COUT), F32),
-            pltpu.VMEM((2, LINES + 8, CIN), F32),
+            pltpu.VMEM((LINES + 8, COLS, COUT), F32),
+            pltpu.VMEM((2, ROWS + 2, COLS, 3 * CIN), BF16),
+            pltpu.VMEM((2, LINES + 16, CIN), BF16),
             pltpu.VMEM((LINES, COLS, CIN), BF16),
         ),
         in_specs=[hbm] * 5,
-        out_specs=(vmem,) * 4,
+        out_specs=(vmem,) * 5,
         scratch_shapes=[
             pltpu.VMEM((CIN, COUT), BF16),
             pltpu.VMEM((1, CIN), F32),
@@ -389,10 +409,10 @@
             pltpu.VMEM((STRIPS + 2, ROWS + 2, COLS, 3 * COUT), BF16),
             pltpu.VMEM((LINES, COLS, CIN), F32),
             pltpu.VMEM((LINES, COLS, CIN), F32),
-            pltpu.VMEM((STRIPS + 2, ROWS + 2, COLS, 3 * CIN), BF16),
-            pltpu.VMEM((8, 32, CIN), F32),
-            pltpu.VMEM((2, CHIPS, 8, CIN), F32),
-            pltpu.VMEM((4 * ROWS * COLS, COUT), F32),
+            pltpu.VMEM((STRIPS, ROWS + 2, COLS, 3 * CIN), BF16),
+            pltpu.VMEM((8, COLS, CIN), F32),
+            pltpu.VMEM((2, LINES, CIN), F32),
+            pltpu.VMEM((2, LINES, CIN), BF16),
             dma((3 + 9,)),
             dma,
             dma((STRIPS - 1,)),
@@ -401,8 +421,8 @@
             dma((2, 2)),
             dma,
             dma,
-            dma((2, CHIPS)),
-            dma((2, CHIPS)),
+            dma((2,)),
+            dma((2,)),
             dma((3,)),
             dma((3,)),
         ],
@@ -425,10 +445,10 @@
             jax.ShapeDtypeStruct((LINES, COLS, COUT), BF16),
             jax.ShapeDtypeStruct((LINES, COLS, CIN), BF16),
         ),
-        in_specs=[vmem] * 4,
+        in_specs=[vmem] * 5,
         out_specs=(hbm, hbm),
         scratch_shapes=[
-            pltpu.VMEM((LINES + 8, 3 * CIN), F32),
+            pltpu.VMEM((2, LINES + 8, 3 * CIN), F32),
             pltpu.VMEM((LINES, COLS, COUT), F32),
             pltpu.VMEM((LINES, COLS, COUT), BF16),
             dma((2,)),

time: 43.3 us -> 42.1 us (0.972)
  the two profiles are of different devices: /device:TPU:68 before, /device:TPU:1 now
where the time goes in v3:
time: 42.1 us; the launch traced here: 42 us
  Pallas kernels  41.4 us (98%)
  between operations  0.64 us (2%)
    pallas_call x1, Pallas kernels, local(): pl.pallas_call(kernel, out_shape=(pltpu.VMEM((9, 3 * CIN, COUT), BF16), p...  39.3 us
    pallas_call x1, Pallas kernels, local(): pl.pallas_call(finish, out_shape=(jax.ShapeDtypeStruct((LINES, COLS, COUT...  2.1 us

profile of v3, /device:TPU:1, one launch (start us, length us, event | category | flops | bytes accessed | tf_op | source)
XLA Modules:
  0.0 42.0 jit_solution(15470514422190477219)
XLA Ops:
  0.6 39.3 %shard_map.68 = (bf16[9,1536,256]{2,1,0:T(8,128)(2,1)S(1)}, f32[72,16,256]{2,1,0:T(8,128)S(1)}, bf16[2,6,16,1536]{3,2,1,0:T(8,128)(2,1)S(1)}, bf16[2,80,512]{2,1,0:T(8,128)(2,1)S(1)}, bf16[64,16,512]{2,1,0:T(8,128)(2,1)S(1)}) custom-call(bf16[4,256,512]{2,1,0:T(8,128)(2,1)} %bitcast.11, f32[1,512]{1,0:T(1,128)} %bitcast.15, bf16[9,1536,256]{2,1,0:T(8,128)(2,1)} %bitcast.10, ...), custom_call_target="tpu_custom_call" | custom-call | flops 15032385536 | bytes 11534336 | tf_op jit(solution)/shard_map/pallas_call | solution.py:388
  39.9 2.1 %shard_map.69 = (bf16[64,16,256]{2,1,0:T(8,128)(2,1)}, bf16[64,16,512]{2,1,0:T(8,128)(2,1)}) custom-call(bf16[9,1536,256]{2,1,0:T(8,128)(2,1)S(1)} %get-tuple-element.9.w, f32[72,16,256]{2,1,0:T(8,128)S(1)} %get-tuple-element.10.acc, bf16[2,6,16,1536]{3,2,1,0:T(8,128)(2,1)S(1)} %get-tuple-element.11.hidp, bf16[2,80,512]{2,1,0:T(8,128)(2,1)S(1)} %get-tuple-element.12.halo, ...), custom_call_target="tpu_custom_call" | custom-call | tf_op jit(solution)/shard_map/pallas_call | solution.py:442

commit v4 on v3

--- a/solution.py
+++ b/solution.py
@@ -58,7 +58,7 @@
     sides = ((0, right, COLS - 1), (1, left, 0))
 
     barrier = pltpu.get_barrier_semaphore()
-    for k in range(1, STRIPS):
+    for k in (8, 7, 9, 6, 10, 5, 11, 4, 12, 3, 13, 2, 14, 1, 15):
         pl.semaphore_signal(
             barrier, inc=1, device_id={"space": lax.rem(me + k, STRIPS)}, device_id_type=MESH
         )
@@ -209,7 +209,7 @@
             def _():
                 strip_copy(me, source, 0).wait_recv()
 
-    def arrive(c):
+    def arrive(c, grad=True):
         half_gain = 0.5 * gain[...]
         for i in range(2):
             rows = pl.ds(c * 8 + ROWS * i, ROWS)
@@ -219,12 +219,24 @@
             hidden = exact.astype(BF16).astype(F32)
             pad[ROWS * i : ROWS * i + ROWS] = hidden.reshape(ROWS, COLS, CIN)
             put_hidden(hid, 2 * c + i, hidden)
-            gu = gh[rows].reshape(ROWS * COLS, CIN) * half_gain * (twice + exact * (2.0 - twice))
-            along = jnp.mean(gu * x, axis=-1, keepdims=True) * (inv * inv)
-            gx = inv * (gu - x * along) + gs[rows].reshape(ROWS * COLS, CIN)
-            gbuf[rows] = gx.astype(BF16).reshape(ROWS, COLS, CIN)
+            if grad:
+                gradient(rows, x, inv, half_gain, twice, exact)
         for slot, _, col in sides:
             edge[slot, pl.ds(c * 8, 8)] = pad[:, col, :]
+
+    def gradient(rows, x, inv, half_gain, twice, exact):
+        gu = gh[rows].reshape(ROWS * COLS, CIN) * half_gain * (twice + exact * (2.0 - twice))
+        along = jnp.mean(gu * x, axis=-1, keepdims=True) * (inv * inv)
+        gx = inv * (gu - x * along) + gs[rows].reshape(ROWS * COLS, CIN)
+        gbuf[rows] = gx.astype(BF16).reshape(ROWS, COLS, CIN)
+
+    def late_gradient(c):
+        half_gain = 0.5 * gain[...]
+        for i in range(2):
+            rows = pl.ds(c * 8 + ROWS * i, ROWS)
+            x = arr[rows].astype(F32).reshape(ROWS * COLS, CIN)
+            inv, half, twice = activate(x, half_gain)
+            gradient(rows, x, inv, half_gain, twice, half * twice)
 
     half = 2 * ROWS * COLS
 
@@ -308,11 +320,12 @@
     last = chip_at(4)
     await_chip(last)
     before[0].start()
-    arrive(last)
+    arrive(last, grad=False)
     for slot in range(2):
         edge_out[slot] = edge[slot].astype(BF16)
     for copy in columns + before[1:]:
         copy.start()
+    late_gradient(last)
     forward([chip_at(3), chip_at(-3), last])
     before[0].wait_recv()
     second = jnp.where(tm == 0, 0.0, 1.0)

time: 42.1 us -> 42 us (level)
  no operation moved by 1% of the time
where the time goes in v4:
time: 42 us; the launch traced here: 41.9 us
  Pallas kernels  41.3 us (98%)
  between operations  0.64 us (2%)
    pallas_call x1, Pallas kernels, local(): pl.pallas_call(kernel, out_shape=(pltpu.VMEM((9, 3 * CIN, COUT), BF16), p...  39.1 us
    pallas_call x1, Pallas kernels, local(): pl.pallas_call(finish, out_shape=(jax.ShapeDtypeStruct((LINES, COLS, COUT...  2.1 us

profile of v4, /device:TPU:1, one launch (start us, length us, event | category | flops | bytes accessed | tf_op | source)
XLA Modules:
  0.0 41.9 jit_solution(11884811898358833095)
XLA Ops:
  0.6 39.1 %shard_map.68 = (bf16[9,1536,256]{2,1,0:T(8,128)(2,1)S(1)}, f32[72,16,256]{2,1,0:T(8,128)S(1)}, bf16[2,6,16,1536]{3,2,1,0:T(8,128)(2,1)S(1)}, bf16[2,80,512]{2,1,0:T(8,128)(2,1)S(1)}, bf16[64,16,512]{2,1,0:T(8,128)(2,1)S(1)}) custom-call(bf16[4,256,512]{2,1,0:T(8,128)(2,1)} %bitcast.11, f32[1,512]{1,0:T(1,128)} %bitcast.15, bf16[9,1536,256]{2,1,0:T(8,128)(2,1)} %bitcast.10, ...), custom_call_target="tpu_custom_call" | custom-call | flops 15032385536 | bytes 11534336 | tf_op jit(solution)/shard_map/pallas_call | solution.py:401
  39.8 2.1 %shard_map.69 = (bf16[64,16,256]{2,1,0:T(8,128)(2,1)}, bf16[64,16,512]{2,1,0:T(8,128)(2,1)}) custom-call(bf16[9,1536,256]{2,1,0:T(8,128)(2,1)S(1)} %get-tuple-element.9.w, f32[72,16,256]{2,1,0:T(8,128)S(1)} %get-tuple-element.10.acc, bf16[2,6,16,1536]{3,2,1,0:T(8,128)(2,1)S(1)} %get-tuple-element.11.hidp, bf16[2,80,512]{2,1,0:T(8,128)(2,1)S(1)} %get-tuple-element.12.halo, ...), custom_call_target="tpu_custom_call" | custom-call | tf_op jit(solution)/shard_map/pallas_call | solution.py:455

commit v5 on v4

--- a/solution.py
+++ b/solution.py
@@ -317,6 +317,7 @@
         return carry
 
     lax.fori_loop(1, 4, pair, 0)
+    forward([chip_at(3)])
     last = chip_at(4)
     await_chip(last)
     before[0].start()
@@ -326,7 +327,7 @@
     for copy in columns + before[1:]:
         copy.start()
     late_gradient(last)
-    forward([chip_at(3), chip_at(-3), last])
+    forward([chip_at(-3), last])
     before[0].wait_recv()
     second = jnp.where(tm == 0, 0.0, 1.0)
     for i in range(2):

time: 42 us -> 42.3 us (level)
  no operation moved by 1% of the time
where the time goes in v5:
time: 42.3 us; the launch traced here: 42.2 us
  Pallas kernels  41.6 us (98%)
  between operations  0.64 us (2%)
    pallas_call x1, Pallas kernels, local(): pl.pallas_call(kernel, out_shape=(pltpu.VMEM((9, 3 * CIN, COUT), BF16), p...  39.5 us
    pallas_call x1, Pallas kernels, local(): pl.pallas_call(finish, out_shape=(jax.ShapeDtypeStruct((LINES, COLS, COUT...  2.1 us

profile of v5, /device:TPU:1, one launch (start us, length us, event | category | flops | bytes accessed | tf_op | source)
XLA Modules:
  0.0 42.2 jit_solution(6810577832183130522)
XLA Ops:
  0.6 39.5 %shard_map.68 = (bf16[9,1536,256]{2,1,0:T(8,128)(2,1)S(1)}, f32[72,16,256]{2,1,0:T(8,128)S(1)}, bf16[2,6,16,1536]{3,2,1,0:T(8,128)(2,1)S(1)}, bf16[2,80,512]{2,1,0:T(8,128)(2,1)S(1)}, bf16[64,16,512]{2,1,0:T(8,128)(2,1)S(1)}) custom-call(bf16[4,256,512]{2,1,0:T(8,128)(2,1)} %bitcast.11, f32[1,512]{1,0:T(1,128)} %bitcast.15, bf16[9,1536,256]{2,1,0:T(8,128)(2,1)} %bitcast.10, ...), custom_call_target="tpu_custom_call" | custom-call | flops 15032385536 | bytes 11534336 | tf_op jit(solution)/shard_map/pallas_call | solution.py:402
  40.1 2.1 %shard_map.69 = (bf16[64,16,256]{2,1,0:T(8,128)(2,1)}, bf16[64,16,512]{2,1,0:T(8,128)(2,1)}) custom-call(bf16[9,1536,256]{2,1,0:T(8,128)(2,1)S(1)} %get-tuple-element.9.w, f32[72,16,256]{2,1,0:T(8,128)S(1)} %get-tuple-element.10.acc, bf16[2,6,16,1536]{3,2,1,0:T(8,128)(2,1)S(1)} %get-tuple-element.11.hidp, bf16[2,80,512]{2,1,0:T(8,128)(2,1)S(1)} %get-tuple-element.12.halo, ...), custom_call_target="tpu_custom_call" | custom-call | tf_op jit(solution)/shard_map/pallas_call | solution.py:456
